TPU v7x, 128 devices: a whole 4x4x4 slice. The times are simulated.
128 devices in a mesh: east: 4 (over y), north: 16 (over x, z), layer: 2 (over core).
Axes of the slice: x: 4, y: 4, z: 4, core: 2. Of those that a mesh axis runs over, the one named last changes fastest.
Arguments:
- head_old: float32 [8, 2048, 1024], P('layer', 'north', 'east'), may hold values from -6 to 6
- head_target: float32 [8, 2048, 1024], P('layer', 'north', 'east'), may hold values from -12 to 12
- conductivity_east: bfloat16 [8, 2048, 1024], P('layer', 'north', 'east'), may hold values from 0.05 to 6, as said below
- conductivity_north: bfloat16 [8, 2048, 1024], P('layer', 'north', 'east'), may hold values from 0.099609375 to 2
- conductivity_vertical: bfloat16 [8, 2048, 1024], P('layer', 'north', 'east'), may hold values from 0.019897461 to 0.5
- storage: bfloat16 [8, 2048, 1024], P('layer', 'north', 'east'), may hold values from 0.19921875 to 2
- well_east: int32 [3000], replicated, may hold values from 0 to 1023
- well_north: int32 [3000], replicated, may hold values from 0 to 2047
- screen_top: int32 [3000], replicated, may hold values from 0 to 3
- screen_bottom: int32 [3000], replicated, may hold values from 3 to 7
- tariff_band: int32 [3000], replicated, may hold values from 0 to 3
- pump_rates: float32 [3000], replicated, may hold values from 0.2 to 2
- ground_level: float32 [3000], replicated, may hold values from 2 to 6
- band_prices: float32 [4], replicated, may hold values from 0.5 to 4
Outputs:
- head_new: float32 [8, 2048, 1024], P('layer', 'north', 'east')
- adjoint_head: float32 [8, 2048, 1024], P('layer', 'north', 'east')
- rate_gradient: float32 [3000], replicated
- pumping_cost: float32 [], replicated
- misfit: float32 [], replicated
Inputs may be any that keep to these rules, and one draw needn't show every extreme that they name: Every screen spans at least one layer: screen_top <= screen_bottom for each well. `conductivity_east`: conductivity along x, positive.
All inputs are finite; a program needn't handle non-finite values.
Results may differ from a plain program's by a relative error of at most 0.0003.
Values may be sent and summed in bfloat16 or wider, within the bound.
A program may use at most 128 MiB of HBM per device.

v0:
```python
import jax
import jax.numpy as jnp
from jax import lax
from jax.sharding import PartitionSpec as P

SWEEPS = 3
CENTRE = 1.0
HALF_WIDTH = 0.95


def extended(value, sides, width):
    for axis, dim in sides:
        size, length = (lax.axis_size(axis), value.shape[dim])
        up = [(i, (i + 1) % size) for i in range(size - 1)]
        down = [(j, i) for i, j in up]
        last = lax.slice_in_dim(value, length - width, length, axis=dim)
        initial = lax.slice_in_dim(value, 0, width, axis=dim)
        before = lax.ppermute(last, axis, up)
        after = lax.ppermute(initial, axis, down)
        value = jnp.concatenate([before, value, after], axis=dim)
    return value


def harmonic(first, second):
    total = first + second
    return 2.0 * first * second / jnp.where(total > 0, total, 1.0)


def face_terms(east_pad, north_pad, up_pad, stored):
    face_east = harmonic(east_pad[:, :, :-1], east_pad[:, :, 1:])
    face_north = harmonic(north_pad[:, :-1], north_pad[:, 1:])
    face_up = harmonic(up_pad[:-1], up_pad[1:])
    diagonal = stored + face_east[:, :, :-1] + face_east[:, :, 1:]
    diagonal = diagonal + face_north[:, :-1] + face_north[:, 1:]
    diagonal = diagonal + face_up[:-1] + face_up[1:]
    positive = diagonal > 0
    inverse = jnp.where(positive, 1.0 / jnp.where(positive, diagonal, 1.0), 0.0)
    return (stored, face_east, face_north, face_up, inverse)


def coefficients(padded_coefs):
    stacked = padded_coefs.astype(jnp.float32)
    east_pad = stacked[0][1:-1, 1:-1, :]
    north_pad = stacked[1][1:-1, :, 1:-1]
    up_pad = stacked[2][:, 1:-1, 1:-1]
    stored = stacked[3][1:-1, 1:-1, 1:-1]
    return face_terms(east_pad, north_pad, up_pad, stored)


def apply_operator(padded, storage_part, face_east, face_north, face_up):
    center = padded[1:-1, 1:-1, 1:-1]
    step_east = padded[1:-1, 1:-1, 1:] - padded[1:-1, 1:-1, :-1]
    step_north = padded[1:-1, 1:, 1:-1] - padded[1:-1, :-1, 1:-1]
    step_up = padded[1:, 1:-1, 1:-1] - padded[:-1, 1:-1, 1:-1]
    flux_east = face_east * step_east
    flux_north = face_north * step_north
    flux_up = face_up * step_up
    total = storage_part * center + (flux_east[:, :, :-1] - flux_east[:, :, 1:])
    total = total + (flux_north[:, :-1] - flux_north[:, 1:])
    return total + (flux_up[:-1] - flux_up[1:])


def keep_whole(field):
    return field


def chebyshev(start, rhs, operate, trim, precondition):
    if start is None:
        residual = rhs
    else:
        residual = trim(rhs) - operate(start)
    direction = precondition(residual) / CENTRE
    if start is None:
        iterate = direction
    else:
        iterate = trim(start) + direction
    sigma = CENTRE / HALF_WIDTH
    factor = 1.0 / sigma
    for sweep_index in range(SWEEPS - 1):
        residual = trim(residual) - operate(direction)
        factor_next = 1.0 / (2.0 * sigma - factor)
        direction = factor_next * factor * trim(
            direction
        ) + 2.0 * factor_next / HALF_WIDTH * precondition(residual)
        iterate = trim(iterate) + direction
        factor = factor_next
    return iterate


def per_device(
    head_old,
    head_target,
    conductivity_east,
    conductivity_north,
    conductivity_vertical,
    storage,
    well_east,
    well_north,
    screen_top,
    screen_bottom,
    tariff_band,
    pump_rates,
    ground_level,
    band_prices,
):
    depth_cells, north_cells, east_cells = head_old.shape
    stacked_coefs = jnp.stack(
        (conductivity_east, conductivity_north, conductivity_vertical, storage)
    )
    padded_coefs = extended(stacked_coefs, (("east", 3), ("north", 2), ("layer", 1)), 1)
    margin = 0
    top_level = coefficients(padded_coefs)
    levels = [None] * (margin + 1)
    levels[margin] = top_level

    def margin_of(field):
        return (field.shape[0] - depth_cells) // 2

    def precondition(residual):
        return levels[margin_of(residual)][4] * residual

    def operate(field):
        padded = extended(field, (("east", 2), ("north", 1), ("layer", 0)), 1)
        level = levels[0]
        return apply_operator(padded, level[0], level[1], level[2], level[3])

    east_start = lax.axis_index("east") * east_cells
    north_start = lax.axis_index("north") * north_cells
    layer_start = lax.axis_index("layer") * depth_cells
    local_east = well_east - east_start
    local_north = well_north - north_start
    owning = (
        (local_east >= 0)
        & (local_east < east_cells)
        & (local_north >= 0)
        & (local_north < north_cells)
    ).astype(jnp.float32)
    cells = jnp.clip(local_north, 0, north_cells - 1) * east_cells + jnp.clip(
        local_east, 0, east_cells - 1
    )
    depth = layer_start + jnp.arange(depth_cells, dtype=jnp.int32)[:, None]
    screened = ((depth >= screen_top[None, :]) & (depth <= screen_bottom[None, :])).astype(
        jnp.float32
    ) * owning[None, :]
    weights = (
        conductivity_east.reshape(depth_cells, north_cells * east_cells)[:, cells].astype(
            jnp.float32
        )
        * screened
    )
    totals = lax.psum(jnp.sum(weights, axis=0), "layer")
    shares = weights / (totals + (1.0 - owning))[None, :]
    flat_shape = (depth_cells, north_cells * east_cells)
    source = (
        jnp.zeros(flat_shape, jnp.float32)
        .at[:, cells]
        .add(pump_rates[None, :] * shares)
        .reshape(head_old.shape)
    )
    stored = storage.astype(jnp.float32)
    rhs = stored * head_old - source
    head_new = chebyshev(head_old, rhs, operate, keep_whole, precondition)
    departure = head_new - head_target
    misfit_part = jnp.sum(departure * departure)
    all_cells = float(
        depth_cells
        * north_cells
        * east_cells
        * lax.axis_size("east")
        * lax.axis_size("north")
        * lax.axis_size("layer")
    )
    head_part = jnp.sum(shares * head_new.reshape(flat_shape)[:, cells], axis=0)
    head_screen, misfit_total = lax.psum((head_part, misfit_part), ("east", "north", "layer"))
    band_ids = jnp.arange(band_prices.shape[0], dtype=jnp.int32)
    prices = jnp.sum(
        jnp.where(tariff_band[:, None] == band_ids[None, :], band_prices[None, :], 0.0), axis=1
    )
    load = (
        departure.reshape(flat_shape)
        .at[:, cells]
        .add(-(prices * pump_rates)[None, :] * shares)
        .reshape(head_old.shape)
    )
    adjoint_head = chebyshev(None, load, operate, keep_whole, precondition)
    adjoint_part = jnp.sum(shares * adjoint_head.reshape(flat_shape)[:, cells], axis=0)
    adjoint_screen = lax.psum(adjoint_part, ("east", "north", "layer"))
    misfit = misfit_total / all_cells
    lift = ground_level - head_screen
    rate_gradient = prices * lift - adjoint_screen
    pumping_cost = jnp.sum(prices * pump_rates * lift)
    return (head_new, adjoint_head, rate_gradient, pumping_cost, misfit)


def solution(mesh):
    in_specs = (
        P("layer", "north", "east"),
        P("layer", "north", "east"),
        P("layer", "north", "east"),
        P("layer", "north", "east"),
        P("layer", "north", "east"),
        P("layer", "north", "east"),
        P(),
        P(),
        P(),
        P(),
        P(),
        P(),
        P(),
        P(),
    )
    out_specs = (P("layer", "north", "east"), P("layer", "north", "east"), P(), P(), P())
    return jax.shard_map(
        per_device, mesh=mesh, in_specs=in_specs, out_specs=out_specs, check_vma=False
    )
```

profile of v0, /device:TPU:1, one launch (start us, length us, event | category | flops | bytes accessed | tf_op | source)
XLA Modules:
  0.0 416.1 jit_solution(4808711370803003127)
XLA Ops:
  0.6 1.9 fusion.86
  2.5 4.0 collective-permute-start.7
  10.5 4.0 collective-permute-start
  15.9 6.1 %copy.26 = bf16[4,128,256]{0,2,1:T(8,128)(2,1)} copy(bf16[4,128,256]{2,1,0:T(8,128)(2,1)S(1)} %copy-done.7) | data formatting | bytes 524288 | tf_op args[2]
  22.1 13.0 %gather_fusion = bf16[3000,4]{1,0:T(8,128)(2,1)S(1)} fusion(bf16[4,32768]{0,1:T(8,128)(2,1)} %bitcast.53, s32[3072]{0:T(1024)S(1)} %pad_clamp_fusion), kind=kCustom, calls=%fused_computation | custom fusion | bytes 60000 | tf_op jit(solution)/shard_map/gather | solution.py:146
  35.2 2.6 fusion.10
  37.8 4.6 %psum.28 = f32[3000]{0:T(1024)S(1)} all-reduce(f32[3000]{0:T(1024)S(1)} %fusion.10), channel_id=1, replica_groups=mesh['east'=4,'north'=16,'layer'=2] {'layer'}, use_global_device_ids=true, to_apply=%region_1.2 | all-reduce | flops 3000 | bytes 24000 | tf_op jit(solution)/shard_map/psum | solution.py:151
  43.4 3.5 collective-permute-start.2
  48.4 4.2 %collective-permute-start.9 = (f32[4,1,258]{2,1,0:T(1,128)S(1)}, f32[4,1,258]{2,1,0:T(1,128)S(1)}, u32[]{:S(2)}, u32[]{:S(2)}) collective-permute-start(f32[4,1,258]{2,1,0:T(1,128)S(1)} %get-tuple-element.54), channel_id=1, source_target_pairs={{0,2},{2,4},{4,6},{6,8},{8,10},{10,12},{12,14},{14,16},{16,18},{18... | collective-permute-start | bytes 12392 | tf_op jit(solution)/shard_map/ppermute | solution.py:18
  53.9 3.4 pad_maximum_fusion
  59.6 4.6 %collective-permute-start.5 = (bf16[4,1,130,258]{3,2,1,0:T(8,128)(2,1)}, bf16[4,1,130,258]{3,2,1,0:T(8,128)(2,1)}, u32[]{:S(2)}, u32[]{:S(2)}) collective-permute-start(bf16[4,1,130,258]{3,2,1,0:T(8,128)(2,1)} %get-tuple-element.33), channel_id=1, source_target_pairs={{1,0},{3,2},{5,4},{7,6},{9,8},{11,10},{13,12},{15,14},{17,16},{19,... | collective-permute-start | bytes 804968 | tf_op jit(solution)/shard_map/ppermute | solution.py:19
  64.1 26.2 %scatter_custom_fusion = f32[4,32768]{0,1:T(8,128)} fusion(s32[3000]{0:T(1024)S(1)} %compare_select_fusion.5, f32[]{:T(128)} %constant.20.clone.1, f32[3000]{0:T(1024)S(1)} %copy-done.20, bf16[3000,4]{1,0:T(8,128)(2,1)S(1)} %gather_fusion, f32[3000]{0:T(1024)S(1)} %subtract_add_fusion, f32[3000]{0:T(1024)S(1)} %and_convert_fusion, s32[4]{0:T(128)S(1)} %iota_add_fusion, ...), kind=kCustom, calls=%fused_computation.5 | custom fusion | flops 108000 | bytes 1354244 | tf_op jit(solution)/shard_map/scatter-add | solution.py:157
  90.4 10.7 %copy.27 = f32[4,128,256]{2,1,0:T(8,128)} copy(f32[4,128,256]{0,2,1:T(8,128)} %bitcast.50) | data formatting | bytes 1048576 | tf_op jit(solution)/shard_map/reshape | solution.py:158
  104.1 5.4 %maximum_convert_fusion = f32[4,6,130,258]{3,2,1,0:T(8,128)S(1)} fusion(bf16[4,1,130,258]{3,2,1,0:T(8,128)(2,1)} %collective-permute-done.5, bf16[4,4,1,258]{3,2,1,0:T(2,128)(2,1)S(1)} %collective-permute-done.3, bf16[4,4,128,1]{3,2,1,0:T(8,128)(2,1)} %collective-permute-done.1, bf16[1,4,128,256]{3,2,1,0:T(8,128)(2,1)S(1)} %bitcast.61, ...), kind=kLoop, calls=%fused_computation.7 | loop fusion | flops 16099200 | bytes 4829760 | tf_op jit(solution)/shard_map/convert_element_type | solution.py:42
  113.0 4.1 collective-permute-start.13
  118.5 3.0 collective-permute-done.13
  121.5 3.8 collective-permute-done.12
  125.5 4.0 collective-permute-start.15
  131.1 2.9 collective-permute-done.14
  134.2 5.5 %collective-permute-start.16 = (f32[1,130,258]{2,1,0:T(8,128)S(1)}, f32[1,130,258]{2,1,0:T(8,128)S(1)}, u32[]{:S(2)}, u32[]{:S(2)}) collective-permute-start(f32[1,130,258]{2,1,0:T(8,128)S(1)} %get-tuple-element.40), channel_id=1, source_target_pairs={{1,0},{3,2},{5,4},{7,6},{9,8},{11,10},{13,12},{15,14},{17,16},{19,... | collective-permute-start | bytes 402488 | tf_op jit(solution)/shard_map/ppermute | solution.py:19
  141.3 1.8 collective-permute-done.17
  144.1 3.6 collective-permute-start.19
  149.0 4.2 %collective-permute-done.19 = f32[4,128,1]{2,1,0:T(8,128)S(1)} collective-permute-done((f32[4,128,1]{2,1,0:T(8,128)S(1)}, f32[4,128,1]{2,1,0:T(8,128)S(1)}, u32[]{:S(2)}, u32[]{:S(2)}) %collective-permute-start.19) | collective-permute-done | bytes 2080 | tf_op jit(solution)/shard_map/ppermute | solution.py:18
  153.2 3.8 collective-permute-done.18
  157.1 3.6 collective-permute-start.21
  162.3 4.9 %collective-permute-done.20 = f32[4,1,258]{2,1,0:T(1,128)S(1)} collective-permute-done((f32[4,1,258]{2,1,0:T(1,128)S(1)}, f32[4,1,258]{2,1,0:T(1,128)S(1)}, u32[]{:S(2)}, u32[]{:S(2)}) %collective-permute-start.20) | collective-permute-done | bytes 4160 | tf_op jit(solution)/shard_map/ppermute | solution.py:19
  167.4 4.3 %collective-permute-start.22 = (f32[1,130,258]{2,1,0:T(8,128)S(1)}, f32[1,130,258]{2,1,0:T(8,128)S(1)}, u32[]{:S(2)}, u32[]{:S(2)}) collective-permute-start(f32[1,130,258]{2,1,0:T(8,128)S(1)} %get-tuple-element.38), channel_id=1, source_target_pairs={{1,0},{3,2},{5,4},{7,6},{9,8},{11,10},{13,12},{15,14},{17,16},{19,... | collective-permute-start | bytes 402488 | tf_op jit(solution)/shard_map/ppermute | solution.py:19
  175.4 2.2 multiply_reduce_fusion
  177.6 9.9 %copy.28 = f32[4,128,256]{0,2,1:T(8,128)} copy(f32[4,128,256]{2,1,0:T(8,128)} %get-tuple-element.11) | data formatting | bytes 1048576 | tf_op jit(solution)/shard_map/sub | solution.py:163
  187.4 31.2 %scatter_custom_fusion.1 = f32[4,32768]{0,1:T(8,128)} fusion(f32[4,32768]{0,1:T(8,128)} %bitcast.48, s32[3000]{0:T(1024)S(1)} %compare_select_fusion.5, f32[3000]{0:T(1024)S(1)} %multiply_negate_fusion, bf16[3000,4]{1,0:T(8,128)(2,1)} %copy-done.4, f32[3000]{0:T(1024)S(1)} %subtract_add_fusion, f32[3000]{0:T(1024)S(1)} %and_convert_fusion, ...), kind=kCustom, calls=%fused_computation.16 | custom fusion | flops 108000 | bytes 1354240 | tf_op jit(solution)/shard_map/scatter-add | solution.py:182
  218.7 10.7 %copy.29 = f32[4,128,256]{2,1,0:T(8,128)} copy(f32[4,128,256]{0,2,1:T(8,128)} %bitcast.49) | data formatting | bytes 1048576 | tf_op jit(solution)/shard_map/reshape | solution.py:183
  230.6 3.2 collective-permute-start.25
  235.1 4.1 collective-permute-done.25
  239.2 3.8 collective-permute-done.24
  243.1 5.7 %collective-permute-start.27 = (f32[4,1,258]{2,1,0:T(1,128)S(1)}, f32[4,1,258]{2,1,0:T(1,128)S(1)}, u32[]{:S(2)}, u32[]{:S(2)}) collective-permute-start(f32[4,1,258]{2,1,0:T(1,128)S(1)} %get-tuple-element.46), channel_id=1, source_target_pairs={{0,2},{2,4},{4,6},{6,8},{8,10},{10,12},{12,14},{14,16},{16,18},{18... | collective-permute-start | bytes 12392 | tf_op jit(solution)/shard_map/ppermute | solution.py:18
  250.5 3.0 collective-permute-done.26
  253.8 4.5 %collective-permute-start.28 = (f32[1,130,258]{2,1,0:T(8,128)S(1)}, f32[1,130,258]{2,1,0:T(8,128)S(1)}, u32[]{:S(2)}, u32[]{:S(2)}) collective-permute-start(f32[1,130,258]{2,1,0:T(8,128)S(1)} %get-tuple-element.36), channel_id=1, source_target_pairs={{1,0},{3,2},{5,4},{7,6},{9,8},{11,10},{13,12},{15,14},{17,16},{19,... | collective-permute-start | bytes 402488 | tf_op jit(solution)/shard_map/ppermute | solution.py:19
  261.9 2.5 multiply_add_fusion
  265.3 1.9 collective-permute-start.31
  268.5 9.7 %copy.31 = f32[4,128,256]{0,2,1:T(8,128)} copy(f32[4,128,256]{2,1,0:T(8,128)} %get-tuple-element.12) | data formatting | bytes 1048576 | tf_op jit(solution)/shard_map/add | solution.py:85
  278.1 16.6 %gather_fusion.1 = f32[3000,4]{1,0:T(8,128)} fusion(f32[4,32768]{0,1:T(8,128)} %bitcast.52, s32[3072]{0:T(1024)S(1)} %pad_clamp_fusion), kind=kCustom, calls=%fused_computation.1 | custom fusion | bytes 108000 | tf_op jit(solution)/shard_map/gather | solution.py:173
  295.6 3.7 collective-permute-start.33
  301.9 2.1 collective-permute-done.32
  305.1 3.5 collective-permute-start.34
  314.0 8.8 %copy.32 = f32[4,128,256]{0,2,1:T(8,128)} copy(f32[4,128,256]{2,1,0:T(8,128)S(1)} %fusion.47) | data formatting | bytes 1048576 | tf_op jit(solution)/shard_map/add | solution.py:85
  322.8 16.7 %gather_fusion.2 = f32[3000,4]{1,0:T(8,128)} fusion(f32[4,32768]{0,1:T(8,128)} %bitcast.51, s32[3072]{0:T(1024)S(1)} %pad_clamp_fusion), kind=kCustom, calls=%fused_computation.2 | custom fusion | bytes 108000 | tf_op jit(solution)/shard_map/gather | solution.py:186
  339.5 5.9 %fusion.3 = (f32[3000]{0:T(1024)S(1)}, f32[3000]{0:T(1024)S(1)}) fusion(f32[3000,4]{1,0:T(8,128)S(1)} %copy-done.16, f32[3000]{0:T(1024)S(1)} %subtract_add_fusion, f32[3000]{0:T(1024)S(1)} %and_convert_fusion, s32[3000]{0:T(1024)S(1)} %copy-done.18, s32[3000]{0:T(1024)S(1)} %copy-done.19, s32[4]{0:T(128)S(1)} %iota_add_fusion, ...), kind=kLoop, calls=%fused_computation.15 | loop fusion | flops 126000 | bytes 192016 | tf_op jit(solution)/shard_map/reduce_sum | solution.py:173
  345.4 67.7 %all-reduce = (f32[3000]{0:T(1024)S(1)}, f32[3000]{0:T(1024)S(1)}, f32[]{:T(128)}) all-reduce(f32[3000]{0:T(1024)S(1)} %get-tuple-element.6, f32[3000]{0:T(1024)S(1)} %get-tuple-element.5, f32[]{:T(128)} %get-tuple-element.10), channel_id=1, replica_groups=mesh['east'=4,'north'=16,'layer'=2] {'east','north','layer'}, use_global_device_ids=true, to_apply=%region_8.9 | all-reduce | flops 6001 | bytes 48008 | tf_op jit(solution)/shard_map/psum | solution.py:187
  (142 shorter events, 51.3 us)
Async XLA Ops:
  2.5 45.7 %collective-permute-start.7 = (f32[4,128,1]{2,1,0:T(8,128)}, f32[4,128,1]{2,1,0:T(8,128)S(1)}, u32[]{:S(2)}, u32[]{:S(2)}) collective-permute-start(f32[4,128,1]{2,1,0:T(8,128)} %get-tuple-element.64), channel_id=1, source_target_pairs={{0,32},{32,64},{64,96},{1,33},{33,65},{65,97},{2,34},{34,66},{66,9... | collective-permute-start | bytes 6152 | tf_op jit(solution)/shard_map/ppermute | solution.py:18
  6.6 41.7 %collective-permute-start.6 = (f32[4,128,1]{2,1,0:T(8,128)}, f32[4,128,1]{2,1,0:T(8,128)S(1)}, u32[]{:S(2)}, u32[]{:S(2)}) collective-permute-start(f32[4,128,1]{2,1,0:T(8,128)} %get-tuple-element.65), channel_id=1, source_target_pairs={{32,0},{64,32},{96,64},{33,1},{65,33},{97,65},{34,2},{66,34},{98,6... | collective-permute-start | bytes 6152 | tf_op jit(solution)/shard_map/ppermute | solution.py:19
  10.5 31.9 %collective-permute-start = (bf16[4,4,128,1]{3,2,1,0:T(8,128)(2,1)}, bf16[4,4,128,1]{3,2,1,0:T(8,128)(2,1)S(1)}, u32[]{:S(2)}, u32[]{:S(2)}) collective-permute-start(bf16[4,4,128,1]{3,2,1,0:T(8,128)(2,1)} %get-tuple-element.52), channel_id=1, source_target_pairs={{0,32},{32,64},{64,96},{1,33},{33,65},{65,97},{2,34},{34,66},{66,9... | collective-permute-start | bytes 12296 | tf_op jit(solution)/shard_map/ppermute | solution.py:18
  14.5 27.9 %collective-permute-start.1 = (bf16[4,4,128,1]{3,2,1,0:T(8,128)(2,1)}, bf16[4,4,128,1]{3,2,1,0:T(8,128)(2,1)}, u32[]{:S(2)}, u32[]{:S(2)}) collective-permute-start(bf16[4,4,128,1]{3,2,1,0:T(8,128)(2,1)} %get-tuple-element.53), channel_id=1, source_target_pairs={{32,0},{64,32},{96,64},{33,1},{65,33},{97,65},{34,2},{66,34},{98,6... | collective-permute-start | bytes 12296 | tf_op jit(solution)/shard_map/ppermute | solution.py:19
  15.9 19.2 %copy-start.18 = (s32[3000]{0:T(1024)S(1)}, s32[3000]{0:T(1024)}, u32[]{:S(2)}) copy-start(s32[3000]{0:T(1024)} %param.23) | copy-start | bytes 36004
  15.9 19.2 %copy-start.19 = (s32[3000]{0:T(1024)S(1)}, s32[3000]{0:T(1024)}, u32[]{:S(2)}) copy-start(s32[3000]{0:T(1024)} %param.22) | copy-start | bytes 36004
  15.9 26.5 %copy-start.8 = (bf16[4,128,256]{2,1,0:T(8,128)(2,1)S(1)}, bf16[4,128,256]{2,1,0:T(8,128)(2,1)}, u32[]{:S(2)}) copy-start(bf16[4,128,256]{2,1,0:T(8,128)(2,1)} %param.19) | copy-start | bytes 786436
  15.9 26.5 %copy-start.10 = (bf16[4,128,256]{2,1,0:T(8,128)(2,1)S(1)}, bf16[4,128,256]{2,1,0:T(8,128)(2,1)}, u32[]{:S(2)}) copy-start(bf16[4,128,256]{2,1,0:T(8,128)(2,1)} %param.18) | copy-start | bytes 786436
  22.1 26.2 %copy-start = (f32[4,128,256]{2,1,0:T(8,128)S(1)}, f32[4,128,256]{2,1,0:T(8,128)}, u32[]{:S(2)}) copy-start(f32[4,128,256]{2,1,0:T(8,128)} %param.14) | copy-start | bytes 1572868
  35.1 29.0 %copy-start.4 = (bf16[3000,4]{1,0:T(8,128)(2,1)}, bf16[3000,4]{1,0:T(8,128)(2,1)S(1)}, u32[]{:S(2)}) copy-start(bf16[3000,4]{1,0:T(8,128)(2,1)S(1)} %gather_fusion) | copy-start | bytes 72004
  43.4 10.5 %collective-permute-start.2 = (bf16[4,4,1,258]{3,2,1,0:T(2,128)(2,1)S(1)}, bf16[4,4,1,258]{3,2,1,0:T(2,128)(2,1)S(1)}, u32[]{:S(2)}, u32[]{:S(2)}) collective-permute-start(bf16[4,4,1,258]{3,2,1,0:T(2,128)(2,1)S(1)} %get-tuple-element.30), channel_id=1, source_target_pairs={{0,2},{2,4},{4,6},{6,8},{8,10},{10,12},{12,14},{14,16},{16,18},{18... | collective-permute-start | bytes 24776 | tf_op jit(solution)/shard_map/ppermute | solution.py:18
  47.0 6.9 %collective-permute-start.3 = (bf16[4,4,1,258]{3,2,1,0:T(2,128)(2,1)S(1)}, bf16[4,4,1,258]{3,2,1,0:T(2,128)(2,1)S(1)}, u32[]{:S(2)}, u32[]{:S(2)}) collective-permute-start(bf16[4,4,1,258]{3,2,1,0:T(2,128)(2,1)S(1)} %get-tuple-element.31), channel_id=1, source_target_pairs={{2,0},{4,2},{6,4},{8,6},{10,8},{12,10},{14,12},{16,14},{18,16},{20... | collective-permute-start | bytes 24776 | tf_op jit(solution)/shard_map/ppermute | solution.py:19
  48.4 52.7 %collective-permute-start.9 = (f32[4,1,258]{2,1,0:T(1,128)S(1)}, f32[4,1,258]{2,1,0:T(1,128)S(1)}, u32[]{:S(2)}, u32[]{:S(2)}) collective-permute-start(f32[4,1,258]{2,1,0:T(1,128)S(1)} %get-tuple-element.54), channel_id=1, source_target_pairs={{0,2},{2,4},{4,6},{6,8},{8,10},{10,12},{12,14},{14,16},{16,18},{18... | collective-permute-start | bytes 12392 | tf_op jit(solution)/shard_map/ppermute | solution.py:18
  52.6 48.5 %collective-permute-start.8 = (f32[4,1,258]{2,1,0:T(1,128)S(1)}, f32[4,1,258]{2,1,0:T(1,128)S(1)}, u32[]{:S(2)}, u32[]{:S(2)}) collective-permute-start(f32[4,1,258]{2,1,0:T(1,128)S(1)} %get-tuple-element.55), channel_id=1, source_target_pairs={{2,0},{4,2},{6,4},{8,6},{10,8},{12,10},{14,12},{16,14},{18,16},{20... | collective-permute-start | bytes 12392 | tf_op jit(solution)/shard_map/ppermute | solution.py:19
  58.3 45.8 %collective-permute-start.4 = (bf16[4,1,130,258]{3,2,1,0:T(8,128)(2,1)}, bf16[4,1,130,258]{3,2,1,0:T(8,128)(2,1)}, u32[]{:S(2)}, u32[]{:S(2)}) collective-permute-start(bf16[4,1,130,258]{3,2,1,0:T(8,128)(2,1)} %get-tuple-element.32), channel_id=1, source_target_pairs={{0,1},{2,3},{4,5},{6,7},{8,9},{10,11},{12,13},{14,15},{16,17},{18,... | collective-permute-start | bytes 804968 | tf_op jit(solution)/shard_map/ppermute | solution.py:18
  59.6 44.5 %collective-permute-start.5 = (bf16[4,1,130,258]{3,2,1,0:T(8,128)(2,1)}, bf16[4,1,130,258]{3,2,1,0:T(8,128)(2,1)}, u32[]{:S(2)}, u32[]{:S(2)}) collective-permute-start(bf16[4,1,130,258]{3,2,1,0:T(8,128)(2,1)} %get-tuple-element.33), channel_id=1, source_target_pairs={{1,0},{3,2},{5,4},{7,6},{9,8},{11,10},{13,12},{15,14},{17,16},{19,... | collective-permute-start | bytes 804968 | tf_op jit(solution)/shard_map/ppermute | solution.py:19
  90.4 13.8 %copy-start.12 = (bf16[4,128,256]{2,1,0:T(8,128)(2,1)S(1)}, bf16[4,128,256]{2,1,0:T(8,128)(2,1)}, u32[]{:S(2)}) copy-start(bf16[4,128,256]{2,1,0:T(8,128)(2,1)} %param.17) | copy-start | bytes 786436
  101.3 9.7 %collective-permute-start.10 = (f32[1,130,258]{2,1,0:T(8,128)S(1)}, f32[1,130,258]{2,1,0:T(8,128)S(1)}, u32[]{:S(2)}, u32[]{:S(2)}) collective-permute-start(f32[1,130,258]{2,1,0:T(8,128)S(1)} %get-tuple-element.42), channel_id=1, source_target_pairs={{1,0},{3,2},{5,4},{7,6},{9,8},{11,10},{13,12},{15,14},{17,16},{19,... | collective-permute-start | bytes 402488 | tf_op jit(solution)/shard_map/ppermute | solution.py:19
  102.6 8.4 %collective-permute-start.11 = (f32[1,130,258]{2,1,0:T(8,128)S(1)}, f32[1,130,258]{2,1,0:T(8,128)S(1)}, u32[]{:S(2)}, u32[]{:S(2)}) collective-permute-start(f32[1,130,258]{2,1,0:T(8,128)S(1)} %get-tuple-element.43), channel_id=1, source_target_pairs={{0,1},{2,3},{4,5},{6,7},{8,9},{10,11},{12,13},{14,15},{16,17},{18,... | collective-permute-start | bytes 402488 | tf_op jit(solution)/shard_map/ppermute | solution.py:18
  109.9 65.5 %copy-start.6 = (f32[6,130,258]{2,1,0:T(8,128)}, f32[6,130,258]{2,1,0:T(8,128)S(1)}, u32[]{:S(2)}) copy-start(f32[6,130,258]{2,1,0:T(8,128)S(1)} %get-tuple-element.26) | copy-start | bytes 2414884
  112.8 116.5 %copy-start.1 = (f32[4,128,256]{2,1,0:T(8,128)}, f32[4,128,256]{2,1,0:T(8,128)S(1)}, u32[]{:S(2)}) copy-start(f32[4,128,256]{2,1,0:T(8,128)S(1)} %get-tuple-element.19) | copy-start | bytes 1572868
  113.0 8.5 %collective-permute-start.13 = (f32[4,128,1]{2,1,0:T(8,128)S(1)}, f32[4,128,1]{2,1,0:T(8,128)S(1)}, u32[]{:S(2)}, u32[]{:S(2)}) collective-permute-start(f32[4,128,1]{2,1,0:T(8,128)S(1)} %get-tuple-element.62), channel_id=1, source_target_pairs={{0,32},{32,64},{64,96},{1,33},{33,65},{65,97},{2,34},{34,66},{66,9... | collective-permute-start | bytes 6152 | tf_op jit(solution)/shard_map/ppermute | solution.py:18
  117.1 8.3 %collective-permute-start.12 = (f32[4,128,1]{2,1,0:T(8,128)S(1)}, f32[4,128,1]{2,1,0:T(8,128)S(1)}, u32[]{:S(2)}, u32[]{:S(2)}) collective-permute-start(f32[4,128,1]{2,1,0:T(8,128)S(1)} %get-tuple-element.63), channel_id=1, source_target_pairs={{32,0},{64,32},{96,64},{33,1},{65,33},{97,65},{34,2},{66,34},{98,6... | collective-permute-start | bytes 6152 | tf_op jit(solution)/shard_map/ppermute | solution.py:19
  125.5 5.6 %collective-permute-start.15 = (f32[4,1,258]{2,1,0:T(1,128)S(1)}, f32[4,1,258]{2,1,0:T(1,128)S(1)}, u32[]{:S(2)}, u32[]{:S(2)}) collective-permute-start(f32[4,1,258]{2,1,0:T(1,128)S(1)} %get-tuple-element.50), channel_id=1, source_target_pairs={{0,2},{2,4},{4,6},{6,8},{8,10},{10,12},{12,14},{14,16},{16,18},{18... | collective-permute-start | bytes 12392 | tf_op jit(solution)/shard_map/ppermute | solution.py:18
  129.5 4.5 %collective-permute-start.14 = (f32[4,1,258]{2,1,0:T(1,128)S(1)}, f32[4,1,258]{2,1,0:T(1,128)S(1)}, u32[]{:S(2)}, u32[]{:S(2)}) collective-permute-start(f32[4,1,258]{2,1,0:T(1,128)S(1)} %get-tuple-element.51), channel_id=1, source_target_pairs={{2,0},{4,2},{6,4},{8,6},{10,8},{12,10},{14,12},{16,14},{18,16},{20... | collective-permute-start | bytes 12392 | tf_op jit(solution)/shard_map/ppermute | solution.py:19
  134.2 7.1 %collective-permute-start.16 = (f32[1,130,258]{2,1,0:T(8,128)S(1)}, f32[1,130,258]{2,1,0:T(8,128)S(1)}, u32[]{:S(2)}, u32[]{:S(2)}) collective-permute-start(f32[1,130,258]{2,1,0:T(8,128)S(1)} %get-tuple-element.40), channel_id=1, source_target_pairs={{1,0},{3,2},{5,4},{7,6},{9,8},{11,10},{13,12},{15,14},{17,16},{19,... | collective-permute-start | bytes 402488 | tf_op jit(solution)/shard_map/ppermute | solution.py:19
  139.7 3.4 collective-permute-start.17
  144.1 9.1 %collective-permute-start.19 = (f32[4,128,1]{2,1,0:T(8,128)S(1)}, f32[4,128,1]{2,1,0:T(8,128)S(1)}, u32[]{:S(2)}, u32[]{:S(2)}) collective-permute-start(f32[4,128,1]{2,1,0:T(8,128)S(1)} %get-tuple-element.60), channel_id=1, source_target_pairs={{0,32},{32,64},{64,96},{1,33},{33,65},{65,97},{2,34},{34,66},{66,9... | collective-permute-start | bytes 6152 | tf_op jit(solution)/shard_map/ppermute | solution.py:18
  147.6 9.3 %collective-permute-start.18 = (f32[4,128,1]{2,1,0:T(8,128)S(1)}, f32[4,128,1]{2,1,0:T(8,128)S(1)}, u32[]{:S(2)}, u32[]{:S(2)}) collective-permute-start(f32[4,128,1]{2,1,0:T(8,128)S(1)} %get-tuple-element.61), channel_id=1, source_target_pairs={{32,0},{64,32},{96,64},{33,1},{65,33},{97,65},{34,2},{66,34},{98,6... | collective-permute-start | bytes 6152 | tf_op jit(solution)/shard_map/ppermute | solution.py:19
  157.1 5.2 %collective-permute-start.21 = (f32[4,1,258]{2,1,0:T(1,128)S(1)}, f32[4,1,258]{2,1,0:T(1,128)S(1)}, u32[]{:S(2)}, u32[]{:S(2)}) collective-permute-start(f32[4,1,258]{2,1,0:T(1,128)S(1)} %get-tuple-element.48), channel_id=1, source_target_pairs={{0,2},{2,4},{4,6},{6,8},{8,10},{10,12},{12,14},{14,16},{16,18},{18... | collective-permute-start | bytes 12392 | tf_op jit(solution)/shard_map/ppermute | solution.py:18
  160.6 6.5 %collective-permute-start.20 = (f32[4,1,258]{2,1,0:T(1,128)S(1)}, f32[4,1,258]{2,1,0:T(1,128)S(1)}, u32[]{:S(2)}, u32[]{:S(2)}) collective-permute-start(f32[4,1,258]{2,1,0:T(1,128)S(1)} %get-tuple-element.49), channel_id=1, source_target_pairs={{2,0},{4,2},{6,4},{8,6},{10,8},{12,10},{14,12},{16,14},{18,16},{20... | collective-permute-start | bytes 12392 | tf_op jit(solution)/shard_map/ppermute | solution.py:19
  167.4 6.1 %collective-permute-start.22 = (f32[1,130,258]{2,1,0:T(8,128)S(1)}, f32[1,130,258]{2,1,0:T(8,128)S(1)}, u32[]{:S(2)}, u32[]{:S(2)}) collective-permute-start(f32[1,130,258]{2,1,0:T(8,128)S(1)} %get-tuple-element.38), channel_id=1, source_target_pairs={{1,0},{3,2},{5,4},{7,6},{9,8},{11,10},{13,12},{15,14},{17,16},{19,... | collective-permute-start | bytes 402488 | tf_op jit(solution)/shard_map/ppermute | solution.py:19
  171.7 3.4 collective-permute-start.23
  230.6 8.6 %collective-permute-start.25 = (f32[4,128,1]{2,1,0:T(8,128)S(1)}, f32[4,128,1]{2,1,0:T(8,128)S(1)}, u32[]{:S(2)}, u32[]{:S(2)}) collective-permute-start(f32[4,128,1]{2,1,0:T(8,128)S(1)} %get-tuple-element.58), channel_id=1, source_target_pairs={{0,32},{32,64},{64,96},{1,33},{33,65},{65,97},{2,34},{34,66},{66,9... | collective-permute-start | bytes 6152 | tf_op jit(solution)/shard_map/ppermute | solution.py:18
  233.8 9.2 %collective-permute-start.24 = (f32[4,128,1]{2,1,0:T(8,128)S(1)}, f32[4,128,1]{2,1,0:T(8,128)S(1)}, u32[]{:S(2)}, u32[]{:S(2)}) collective-permute-start(f32[4,128,1]{2,1,0:T(8,128)S(1)} %get-tuple-element.59), channel_id=1, source_target_pairs={{32,0},{64,32},{96,64},{33,1},{65,33},{97,65},{34,2},{66,34},{98,6... | collective-permute-start | bytes 6152 | tf_op jit(solution)/shard_map/ppermute | solution.py:19
  243.1 7.4 %collective-permute-start.27 = (f32[4,1,258]{2,1,0:T(1,128)S(1)}, f32[4,1,258]{2,1,0:T(1,128)S(1)}, u32[]{:S(2)}, u32[]{:S(2)}) collective-permute-start(f32[4,1,258]{2,1,0:T(1,128)S(1)} %get-tuple-element.46), channel_id=1, source_target_pairs={{0,2},{2,4},{4,6},{6,8},{8,10},{10,12},{12,14},{14,16},{16,18},{18... | collective-permute-start | bytes 12392 | tf_op jit(solution)/shard_map/ppermute | solution.py:18
  248.9 4.7 %collective-permute-start.26 = (f32[4,1,258]{2,1,0:T(1,128)S(1)}, f32[4,1,258]{2,1,0:T(1,128)S(1)}, u32[]{:S(2)}, u32[]{:S(2)}) collective-permute-start(f32[4,1,258]{2,1,0:T(1,128)S(1)} %get-tuple-element.47), channel_id=1, source_target_pairs={{2,0},{4,2},{6,4},{8,6},{10,8},{12,10},{14,12},{16,14},{18,16},{20... | collective-permute-start | bytes 12392 | tf_op jit(solution)/shard_map/ppermute | solution.py:19
  253.8 6.0 %collective-permute-start.28 = (f32[1,130,258]{2,1,0:T(8,128)S(1)}, f32[1,130,258]{2,1,0:T(8,128)S(1)}, u32[]{:S(2)}, u32[]{:S(2)}) collective-permute-start(f32[1,130,258]{2,1,0:T(8,128)S(1)} %get-tuple-element.36), channel_id=1, source_target_pairs={{1,0},{3,2},{5,4},{7,6},{9,8},{11,10},{13,12},{15,14},{17,16},{19,... | collective-permute-start | bytes 402488 | tf_op jit(solution)/shard_map/ppermute | solution.py:19
  258.2 3.4 collective-permute-start.29
  265.3 29.5 %collective-permute-start.31 = (f32[4,128,1]{2,1,0:T(8,128)}, f32[4,128,1]{2,1,0:T(8,128)S(1)}, u32[]{:S(2)}, u32[]{:S(2)}) collective-permute-start(f32[4,128,1]{2,1,0:T(8,128)} %get-tuple-element.56), channel_id=1, source_target_pairs={{0,32},{32,64},{64,96},{1,33},{33,65},{65,97},{2,34},{34,66},{66,9... | collective-permute-start | bytes 6152 | tf_op jit(solution)/shard_map/ppermute | solution.py:18
  267.2 27.6 %collective-permute-start.30 = (f32[4,128,1]{2,1,0:T(8,128)}, f32[4,128,1]{2,1,0:T(8,128)}, u32[]{:S(2)}, u32[]{:S(2)}) collective-permute-start(f32[4,128,1]{2,1,0:T(8,128)} %get-tuple-element.57), channel_id=1, source_target_pairs={{32,0},{64,32},{96,64},{33,1},{65,33},{97,65},{34,2},{66,34},{98,6... | collective-permute-start | bytes 6152 | tf_op jit(solution)/shard_map/ppermute | solution.py:19
  295.6 6.3 %collective-permute-start.33 = (f32[4,1,258]{2,1,0:T(1,128)S(1)}, f32[4,1,258]{2,1,0:T(1,128)S(1)}, u32[]{:S(2)}, u32[]{:S(2)}) collective-permute-start(f32[4,1,258]{2,1,0:T(1,128)S(1)} %get-tuple-element.44), channel_id=1, source_target_pairs={{0,2},{2,4},{4,6},{6,8},{8,10},{10,12},{12,14},{14,16},{16,18},{18... | collective-permute-start | bytes 12392 | tf_op jit(solution)/shard_map/ppermute | solution.py:18
  299.3 4.7 %collective-permute-start.32 = (f32[4,1,258]{2,1,0:T(1,128)S(1)}, f32[4,1,258]{2,1,0:T(1,128)S(1)}, u32[]{:S(2)}, u32[]{:S(2)}) collective-permute-start(f32[4,1,258]{2,1,0:T(1,128)S(1)} %get-tuple-element.45), channel_id=1, source_target_pairs={{2,0},{4,2},{6,4},{8,6},{10,8},{12,10},{14,12},{16,14},{18,16},{20... | collective-permute-start | bytes 12392 | tf_op jit(solution)/shard_map/ppermute | solution.py:19
  305.1 5.1 %collective-permute-start.34 = (f32[1,130,258]{2,1,0:T(8,128)S(1)}, f32[1,130,258]{2,1,0:T(8,128)S(1)}, u32[]{:S(2)}, u32[]{:S(2)}) collective-permute-start(f32[1,130,258]{2,1,0:T(8,128)S(1)} %get-tuple-element.34), channel_id=1, source_target_pairs={{1,0},{3,2},{5,4},{7,6},{9,8},{11,10},{13,12},{15,14},{17,16},{19,... | collective-permute-start | bytes 402488 | tf_op jit(solution)/shard_map/ppermute | solution.py:19
  308.6 3.4 collective-permute-start.35
  314.0 25.5 %copy-start.5 = (bf16[3000,4]{1,0:T(8,128)(2,1)S(1)}, bf16[3000,4]{1,0:T(8,128)(2,1)}, u32[]{:S(2)}) copy-start(bf16[3000,4]{1,0:T(8,128)(2,1)} %copy-done.4) | copy-start | bytes 72004
  314.0 25.5 %copy-start.16 = (f32[3000,4]{1,0:T(8,128)S(1)}, f32[3000,4]{1,0:T(8,128)}, u32[]{:S(2)}) copy-start(f32[3000,4]{1,0:T(8,128)} %gather_fusion.1) | copy-start | bytes 144004
  339.5 74.3 %copy-start.23 = (f32[3000]{0:T(1024)S(1)}, f32[3000]{0:T(1024)}, u32[]{:S(2)}) copy-start(f32[3000]{0:T(1024)} %param.26) | copy-start | bytes 36004
  (14 other events, 75.1 us)
where the time goes:
time: 419 us; the launch traced here: 416 us
  local copies, waits for them, and re-layouts  108 us (26%)
  other arithmetic  96.3 us (23%)
  starting transfers between devices  92.9 us (22%)
  blocking collectives  72.3 us (17%)
  waiting for transfers between devices  42.8 us (10%)
    psum x1, blocking collectives, per_device(): adjoint_screen = lax.psum(adjoint_part, ('east', 'north', 'layer'))  67.7 us
    ppermute x18, starting transfers between devices, extended(): before = lax.ppermute(last, axis, up)  53.7 us
    ppermute x18, starting transfers between devices, extended(): after = lax.ppermute(initial, axis, down)  39.2 us
    scatter-add x1, other arithmetic, per_device(): load = departure.reshape(flat_shape).at[:, cells].add(-(prices * pump_rat...  31.2 us
    scatter-add x1, other arithmetic, per_device(): source = jnp.zeros(flat_shape, jnp.float32).at[:, cells].add(pump_rates[N...  26.2 us
    ppermute x18, waiting for transfers between devices, extended(): after = lax.ppermute(initial, axis, down)  24.5 us
    add x2, local copies, waits for them, and re-layouts, chebyshev(): iterate = trim(iterate) + direction  18.4 us
    ppermute x18, waiting for transfers between devices, extended(): before = lax.ppermute(last, axis, up)  18.3 us
  transfers between devices with their start and end apart: 36, of which 14 were waited for; matrix products, arithmetic and copies ran while one was open for 25% of the time, Pallas kernels for 0%

commit v1 on v0

--- a/solution.py
+++ b/solution.py
@@ -184,7 +184,9 @@
     )
     adjoint_head = chebyshev(None, load, operate, keep_whole, precondition)
     adjoint_part = jnp.sum(shares * adjoint_head.reshape(flat_shape)[:, cells], axis=0)
-    adjoint_screen = lax.psum(adjoint_part, ("east", "north", "layer"))
+    adjoint_screen = adjoint_part
+    for over in ("east", ("north", "layer")):
+        adjoint_screen = lax.psum(adjoint_screen, over)
     misfit = misfit_total / all_cells
     lift = ground_level - head_screen
     rate_gradient = prices * lift - adjoint_screen

time: 419 us -> 553 us (1.32)
  blocking collectives: 72.3 us -> 207 us
    psum x1 -> x3, blocking collectives: 67.7 us -> 202 us  [the longest x2 135 us: per_device(): adjoint_screen = lax.psum(adjoint_screen, over)]
  transfers between devices with their start and end apart: 36 -> 36, of which waited for: 14 -> 14; matrix products, arithmetic and copies ran while one was open for 25% -> 19% of each run, Pallas kernels for 0% -> 0%
where the time goes in v1:
time: 553 us; the launch traced here: 551 us
  blocking collectives  207 us (37%)
  local copies, waits for them, and re-layouts  108 us (20%)
  other arithmetic  96.3 us (17%)
  starting transfers between devices  92.9 us (17%)
  waiting for transfers between devices  42.8 us (8%)
    psum x2, blocking collectives, per_device(): adjoint_screen = lax.psum(adjoint_screen, over)  135 us
    psum x1, blocking collectives, per_device(): lax.psum((head_part, misfit_part), ('east', 'north', 'layer'))  67.4 us
    ppermute x18, starting transfers between devices, extended(): before = lax.ppermute(last, axis, up)  53.7 us
    ppermute x18, starting transfers between devices, extended(): after = lax.ppermute(initial, axis, down)  39.2 us
    scatter-add x1, other arithmetic, per_device(): load = departure.reshape(flat_shape).at[:, cells].add(-(prices * pump_rat...  31.2 us
    scatter-add x1, other arithmetic, per_device(): source = jnp.zeros(flat_shape, jnp.float32).at[:, cells].add(pump_rates[N...  26.2 us
    ppermute x18, waiting for transfers between devices, extended(): after = lax.ppermute(initial, axis, down)  24.5 us
    add x2, local copies, waits for them, and re-layouts, chebyshev(): iterate = trim(iterate) + direction  18.5 us
  transfers between devices with their start and end apart: 36, of which 14 were waited for; matrix products, arithmetic and copies ran while one was open for 19% of the time, Pallas kernels for 0%

profile of v1, /device:TPU:1, one launch (start us, length us, event | category | flops | bytes accessed | tf_op | source)
XLA Modules:
  0.0 550.9 jit_solution(9204657253975425472)
XLA Ops:
  2.5 4.0 collective-permute-start.7
  10.5 4.0 collective-permute-start
  15.9 6.2 %copy.26 = bf16[4,128,256]{0,2,1:T(8,128)(2,1)} copy(bf16[4,128,256]{2,1,0:T(8,128)(2,1)S(1)} %copy-done.7) | data formatting | bytes 524288 | tf_op args[2]
  22.1 13.0 %gather_fusion = bf16[3000,4]{1,0:T(8,128)(2,1)S(1)} fusion(bf16[4,32768]{0,1:T(8,128)(2,1)} %bitcast.53, s32[3072]{0:T(1024)S(1)} %pad_clamp_fusion), kind=kCustom, calls=%fused_computation | custom fusion | bytes 60000 | tf_op jit(solution)/shard_map/gather | solution.py:146
  35.2 2.6 fusion.10
  37.8 4.6 psum.35
  43.5 3.5 collective-permute-start.2
  48.5 4.2 collective-permute-start.9
  54.0 3.4 pad_maximum_fusion
  59.6 4.5 collective-permute-start.5
  64.2 26.2 %scatter_custom_fusion = f32[4,32768]{0,1:T(8,128)} fusion(s32[3000]{0:T(1024)S(1)} %compare_select_fusion.5, f32[]{:T(128)} %constant.20.clone.1, f32[3000]{0:T(1024)S(1)} %copy-done.20, bf16[3000,4]{1,0:T(8,128)(2,1)S(1)} %gather_fusion, f32[3000]{0:T(1024)S(1)} %subtract_add_fusion, f32[3000]{0:T(1024)S(1)} %and_convert_fusion, s32[4]{0:T(128)S(1)} %iota_add_fusion, ...), kind=kCustom, calls=%fused_computation.5 | custom fusion | flops 108000 | bytes 1354244 | tf_op jit(solution)/shard_map/scatter-add | solution.py:157
  90.4 10.7 %copy.27 = f32[4,128,256]{2,1,0:T(8,128)} copy(f32[4,128,256]{0,2,1:T(8,128)} %bitcast.50) | data formatting | bytes 1048576 | tf_op jit(solution)/shard_map/reshape | solution.py:158
  104.2 5.4 maximum_convert_fusion
  113.0 4.1 collective-permute-start.13
  118.6 3.0 collective-permute-done.13
  121.6 3.8 collective-permute-done.12
  125.5 4.0 collective-permute-start.15
  131.1 2.9 collective-permute-done.14
  134.3 5.5 %collective-permute-start.16 = (f32[1,130,258]{2,1,0:T(8,128)S(1)}, f32[1,130,258]{2,1,0:T(8,128)S(1)}, u32[]{:S(2)}, u32[]{:S(2)}) collective-permute-start(f32[1,130,258]{2,1,0:T(8,128)S(1)} %get-tuple-element.39), channel_id=1, source_target_pairs={{1,0},{3,2},{5,4},{7,6},{9,8},{11,10},{13,12},{15,14},{17,16},{19,... | collective-permute-start | bytes 402488 | tf_op jit(solution)/shard_map/ppermute | solution.py:19
  144.1 3.6 collective-permute-start.19
  149.0 4.2 collective-permute-done.19
  153.2 3.8 collective-permute-done.18
  157.1 3.6 collective-permute-start.21
  162.3 4.9 collective-permute-done.20
  167.4 4.3 collective-permute-start.22
  175.4 2.2 multiply_reduce_fusion
  177.6 9.8 %copy.28 = f32[4,128,256]{0,2,1:T(8,128)} copy(f32[4,128,256]{2,1,0:T(8,128)} %get-tuple-element.10) | data formatting | bytes 1048576 | tf_op jit(solution)/shard_map/sub | solution.py:163
  187.4 31.2 %scatter_custom_fusion.1 = f32[4,32768]{0,1:T(8,128)} fusion(f32[4,32768]{0,1:T(8,128)} %bitcast.48, s32[3000]{0:T(1024)S(1)} %compare_select_fusion.5, f32[3000]{0:T(1024)S(1)} %multiply_negate_fusion, bf16[3000,4]{1,0:T(8,128)(2,1)} %copy-done.4, f32[3000]{0:T(1024)S(1)} %subtract_add_fusion, f32[3000]{0:T(1024)S(1)} %and_convert_fusion, ...), kind=kCustom, calls=%fused_computation.16 | custom fusion | flops 108000 | bytes 1354240 | tf_op jit(solution)/shard_map/scatter-add | solution.py:182
  218.7 10.7 %copy.29 = f32[4,128,256]{2,1,0:T(8,128)} copy(f32[4,128,256]{0,2,1:T(8,128)} %bitcast.49) | data formatting | bytes 1048576 | tf_op jit(solution)/shard_map/reshape | solution.py:183
  230.6 3.2 collective-permute-start.25
  235.1 4.1 collective-permute-done.25
  239.2 3.8 collective-permute-done.24
  243.1 5.7 %collective-permute-start.27 = (f32[4,1,258]{2,1,0:T(1,128)S(1)}, f32[4,1,258]{2,1,0:T(1,128)S(1)}, u32[]{:S(2)}, u32[]{:S(2)}) collective-permute-start(f32[4,1,258]{2,1,0:T(1,128)S(1)} %get-tuple-element.45), channel_id=1, source_target_pairs={{0,2},{2,4},{4,6},{6,8},{8,10},{10,12},{12,14},{14,16},{16,18},{18... | collective-permute-start | bytes 12392 | tf_op jit(solution)/shard_map/ppermute | solution.py:18
  250.5 3.1 collective-permute-done.26
  253.8 4.5 collective-permute-start.28
  261.9 2.5 multiply_add_fusion
  265.3 1.9 collective-permute-start.31
  268.5 9.7 %copy.31 = f32[4,128,256]{0,2,1:T(8,128)} copy(f32[4,128,256]{2,1,0:T(8,128)} %get-tuple-element.11) | data formatting | bytes 1048576 | tf_op jit(solution)/shard_map/add | solution.py:85
  278.2 16.6 %gather_fusion.1 = f32[3000,4]{1,0:T(8,128)} fusion(f32[4,32768]{0,1:T(8,128)} %bitcast.52, s32[3072]{0:T(1024)S(1)} %pad_clamp_fusion), kind=kCustom, calls=%fused_computation.1 | custom fusion | bytes 108000 | tf_op jit(solution)/shard_map/gather | solution.py:173
  295.7 3.7 collective-permute-start.33
  302.0 2.1 collective-permute-done.32
  305.2 3.5 collective-permute-start.34
  314.1 8.7 %copy.32 = f32[4,128,256]{0,2,1:T(8,128)} copy(f32[4,128,256]{2,1,0:T(8,128)S(1)} %fusion.47) | data formatting | bytes 1048576 | tf_op jit(solution)/shard_map/add | solution.py:85
  322.9 16.7 %gather_fusion.2 = f32[3000,4]{1,0:T(8,128)} fusion(f32[4,32768]{0,1:T(8,128)} %bitcast.51, s32[3072]{0:T(1024)S(1)} %pad_clamp_fusion), kind=kCustom, calls=%fused_computation.2 | custom fusion | bytes 108000 | tf_op jit(solution)/shard_map/gather | solution.py:186
  339.5 5.9 %fusion.3 = (f32[3000]{0:T(1024)S(1)}, f32[3000]{0:T(1024)S(1)}) fusion(f32[3000,4]{1,0:T(8,128)S(1)} %copy-done.16, f32[3000]{0:T(1024)S(1)} %subtract_add_fusion, f32[3000]{0:T(1024)S(1)} %and_convert_fusion, s32[3000]{0:T(1024)S(1)} %copy-done.18, s32[3000]{0:T(1024)S(1)} %copy-done.19, s32[4]{0:T(128)S(1)} %iota_add_fusion, ...), kind=kLoop, calls=%fused_computation.15 | loop fusion | flops 126000 | bytes 192016 | tf_op jit(solution)/shard_map/reduce_sum | solution.py:173
  345.5 13.0 %psum.37 = f32[3000]{0:T(1024)S(1)} all-reduce(f32[3000]{0:T(1024)S(1)} %get-tuple-element.6), channel_id=1, replica_groups=mesh['east'=4,'north'=16,'layer'=2] {'east'}, use_global_device_ids=true, to_apply=%region_8.9 | all-reduce | flops 3000 | bytes 24000 | tf_op jit(solution)/shard_map/psum | solution.py:189
  358.4 122.1 %psum.38 = f32[3000]{0:T(1024)S(1)} all-reduce(f32[3000]{0:T(1024)S(1)} %psum.37), channel_id=1, replica_groups=mesh['east'=4,'north'=16,'layer'=2] {'north','layer'}, use_global_device_ids=true, to_apply=%region_9.10 | all-reduce | flops 3000 | bytes 24000 | tf_op jit(solution)/shard_map/psum | solution.py:189
  480.5 67.4 %all-reduce = (f32[3000]{0:T(1024)S(1)}, f32[]{:T(128)}) all-reduce(f32[3000]{0:T(1024)S(1)} %get-tuple-element.5, f32[]{:T(128)} %get-tuple-element.9), channel_id=1, replica_groups=mesh['east'=4,'north'=16,'layer'=2] {'east','north','layer'}, use_global_device_ids=true, to_apply=%region_6.7 | all-reduce | flops 3001 | bytes 24008 | tf_op jit(solution)/shard_map/psum | solution.py:174
  (144 shorter events, 55.1 us)
Async XLA Ops:
  2.5 45.8 %collective-permute-start.7 = (f32[4,128,1]{2,1,0:T(8,128)}, f32[4,128,1]{2,1,0:T(8,128)S(1)}, u32[]{:S(2)}, u32[]{:S(2)}) collective-permute-start(f32[4,128,1]{2,1,0:T(8,128)} %get-tuple-element.63), channel_id=1, source_target_pairs={{0,32},{32,64},{64,96},{1,33},{33,65},{65,97},{2,34},{34,66},{66,9... | collective-permute-start | bytes 6152 | tf_op jit(solution)/shard_map/ppermute | solution.py:18
  6.6 41.8 %collective-permute-start.6 = (f32[4,128,1]{2,1,0:T(8,128)}, f32[4,128,1]{2,1,0:T(8,128)S(1)}, u32[]{:S(2)}, u32[]{:S(2)}) collective-permute-start(f32[4,128,1]{2,1,0:T(8,128)} %get-tuple-element.64), channel_id=1, source_target_pairs={{32,0},{64,32},{96,64},{33,1},{65,33},{97,65},{34,2},{66,34},{98,6... | collective-permute-start | bytes 6152 | tf_op jit(solution)/shard_map/ppermute | solution.py:19
  10.5 32.0 %collective-permute-start = (bf16[4,4,128,1]{3,2,1,0:T(8,128)(2,1)}, bf16[4,4,128,1]{3,2,1,0:T(8,128)(2,1)S(1)}, u32[]{:S(2)}, u32[]{:S(2)}) collective-permute-start(bf16[4,4,128,1]{3,2,1,0:T(8,128)(2,1)} %get-tuple-element.51), channel_id=1, source_target_pairs={{0,32},{32,64},{64,96},{1,33},{33,65},{65,97},{2,34},{34,66},{66,9... | collective-permute-start | bytes 12296 | tf_op jit(solution)/shard_map/ppermute | solution.py:18
  14.5 28.0 %collective-permute-start.1 = (bf16[4,4,128,1]{3,2,1,0:T(8,128)(2,1)}, bf16[4,4,128,1]{3,2,1,0:T(8,128)(2,1)}, u32[]{:S(2)}, u32[]{:S(2)}) collective-permute-start(bf16[4,4,128,1]{3,2,1,0:T(8,128)(2,1)} %get-tuple-element.52), channel_id=1, source_target_pairs={{32,0},{64,32},{96,64},{33,1},{65,33},{97,65},{34,2},{66,34},{98,6... | collective-permute-start | bytes 12296 | tf_op jit(solution)/shard_map/ppermute | solution.py:19
  15.9 19.3 %copy-start.18 = (s32[3000]{0:T(1024)S(1)}, s32[3000]{0:T(1024)}, u32[]{:S(2)}) copy-start(s32[3000]{0:T(1024)} %param.23) | copy-start | bytes 36004
  15.9 19.3 %copy-start.19 = (s32[3000]{0:T(1024)S(1)}, s32[3000]{0:T(1024)}, u32[]{:S(2)}) copy-start(s32[3000]{0:T(1024)} %param.22) | copy-start | bytes 36004
  15.9 26.6 %copy-start.8 = (bf16[4,128,256]{2,1,0:T(8,128)(2,1)S(1)}, bf16[4,128,256]{2,1,0:T(8,128)(2,1)}, u32[]{:S(2)}) copy-start(bf16[4,128,256]{2,1,0:T(8,128)(2,1)} %param.19) | copy-start | bytes 786436
  15.9 26.6 %copy-start.10 = (bf16[4,128,256]{2,1,0:T(8,128)(2,1)S(1)}, bf16[4,128,256]{2,1,0:T(8,128)(2,1)}, u32[]{:S(2)}) copy-start(bf16[4,128,256]{2,1,0:T(8,128)(2,1)} %param.18) | copy-start | bytes 786436
  22.1 26.2 %copy-start = (f32[4,128,256]{2,1,0:T(8,128)S(1)}, f32[4,128,256]{2,1,0:T(8,128)}, u32[]{:S(2)}) copy-start(f32[4,128,256]{2,1,0:T(8,128)} %param.14) | copy-start | bytes 1572868
  35.2 29.0 %copy-start.4 = (bf16[3000,4]{1,0:T(8,128)(2,1)}, bf16[3000,4]{1,0:T(8,128)(2,1)S(1)}, u32[]{:S(2)}) copy-start(bf16[3000,4]{1,0:T(8,128)(2,1)S(1)} %gather_fusion) | copy-start | bytes 72004
  43.5 10.5 %collective-permute-start.2 = (bf16[4,4,1,258]{3,2,1,0:T(2,128)(2,1)S(1)}, bf16[4,4,1,258]{3,2,1,0:T(2,128)(2,1)S(1)}, u32[]{:S(2)}, u32[]{:S(2)}) collective-permute-start(bf16[4,4,1,258]{3,2,1,0:T(2,128)(2,1)S(1)} %get-tuple-element.29), channel_id=1, source_target_pairs={{0,2},{2,4},{4,6},{6,8},{8,10},{10,12},{12,14},{14,16},{16,18},{18... | collective-permute-start | bytes 24776 | tf_op jit(solution)/shard_map/ppermute | solution.py:18
  47.0 6.9 %collective-permute-start.3 = (bf16[4,4,1,258]{3,2,1,0:T(2,128)(2,1)S(1)}, bf16[4,4,1,258]{3,2,1,0:T(2,128)(2,1)S(1)}, u32[]{:S(2)}, u32[]{:S(2)}) collective-permute-start(bf16[4,4,1,258]{3,2,1,0:T(2,128)(2,1)S(1)} %get-tuple-element.30), channel_id=1, source_target_pairs={{2,0},{4,2},{6,4},{8,6},{10,8},{12,10},{14,12},{16,14},{18,16},{20... | collective-permute-start | bytes 24776 | tf_op jit(solution)/shard_map/ppermute | solution.py:19
  48.5 52.7 %collective-permute-start.9 = (f32[4,1,258]{2,1,0:T(1,128)S(1)}, f32[4,1,258]{2,1,0:T(1,128)S(1)}, u32[]{:S(2)}, u32[]{:S(2)}) collective-permute-start(f32[4,1,258]{2,1,0:T(1,128)S(1)} %get-tuple-element.53), channel_id=1, source_target_pairs={{0,2},{2,4},{4,6},{6,8},{8,10},{10,12},{12,14},{14,16},{16,18},{18... | collective-permute-start | bytes 12392 | tf_op jit(solution)/shard_map/ppermute | solution.py:18
  52.6 48.5 %collective-permute-start.8 = (f32[4,1,258]{2,1,0:T(1,128)S(1)}, f32[4,1,258]{2,1,0:T(1,128)S(1)}, u32[]{:S(2)}, u32[]{:S(2)}) collective-permute-start(f32[4,1,258]{2,1,0:T(1,128)S(1)} %get-tuple-element.54), channel_id=1, source_target_pairs={{2,0},{4,2},{6,4},{8,6},{10,8},{12,10},{14,12},{16,14},{18,16},{20... | collective-permute-start | bytes 12392 | tf_op jit(solution)/shard_map/ppermute | solution.py:19
  58.3 45.8 %collective-permute-start.4 = (bf16[4,1,130,258]{3,2,1,0:T(8,128)(2,1)}, bf16[4,1,130,258]{3,2,1,0:T(8,128)(2,1)}, u32[]{:S(2)}, u32[]{:S(2)}) collective-permute-start(bf16[4,1,130,258]{3,2,1,0:T(8,128)(2,1)} %get-tuple-element.31), channel_id=1, source_target_pairs={{0,1},{2,3},{4,5},{6,7},{8,9},{10,11},{12,13},{14,15},{16,17},{18,... | collective-permute-start | bytes 804968 | tf_op jit(solution)/shard_map/ppermute | solution.py:18
  59.6 44.5 %collective-permute-start.5 = (bf16[4,1,130,258]{3,2,1,0:T(8,128)(2,1)}, bf16[4,1,130,258]{3,2,1,0:T(8,128)(2,1)}, u32[]{:S(2)}, u32[]{:S(2)}) collective-permute-start(bf16[4,1,130,258]{3,2,1,0:T(8,128)(2,1)} %get-tuple-element.32), channel_id=1, source_target_pairs={{1,0},{3,2},{5,4},{7,6},{9,8},{11,10},{13,12},{15,14},{17,16},{19,... | collective-permute-start | bytes 804968 | tf_op jit(solution)/shard_map/ppermute | solution.py:19
  90.4 13.8 %copy-start.12 = (bf16[4,128,256]{2,1,0:T(8,128)(2,1)S(1)}, bf16[4,128,256]{2,1,0:T(8,128)(2,1)}, u32[]{:S(2)}) copy-start(bf16[4,128,256]{2,1,0:T(8,128)(2,1)} %param.17) | copy-start | bytes 786436
  101.4 9.7 %collective-permute-start.10 = (f32[1,130,258]{2,1,0:T(8,128)S(1)}, f32[1,130,258]{2,1,0:T(8,128)S(1)}, u32[]{:S(2)}, u32[]{:S(2)}) collective-permute-start(f32[1,130,258]{2,1,0:T(8,128)S(1)} %get-tuple-element.41), channel_id=1, source_target_pairs={{1,0},{3,2},{5,4},{7,6},{9,8},{11,10},{13,12},{15,14},{17,16},{19,... | collective-permute-start | bytes 402488 | tf_op jit(solution)/shard_map/ppermute | solution.py:19
  102.7 8.4 %collective-permute-start.11 = (f32[1,130,258]{2,1,0:T(8,128)S(1)}, f32[1,130,258]{2,1,0:T(8,128)S(1)}, u32[]{:S(2)}, u32[]{:S(2)}) collective-permute-start(f32[1,130,258]{2,1,0:T(8,128)S(1)} %get-tuple-element.42), channel_id=1, source_target_pairs={{0,1},{2,3},{4,5},{6,7},{8,9},{10,11},{12,13},{14,15},{16,17},{18,... | collective-permute-start | bytes 402488 | tf_op jit(solution)/shard_map/ppermute | solution.py:18
  109.9 65.5 %copy-start.6 = (f32[6,130,258]{2,1,0:T(8,128)}, f32[6,130,258]{2,1,0:T(8,128)S(1)}, u32[]{:S(2)}) copy-start(f32[6,130,258]{2,1,0:T(8,128)S(1)} %get-tuple-element.25) | copy-start | bytes 2414884
  112.9 116.5 %copy-start.1 = (f32[4,128,256]{2,1,0:T(8,128)}, f32[4,128,256]{2,1,0:T(8,128)S(1)}, u32[]{:S(2)}) copy-start(f32[4,128,256]{2,1,0:T(8,128)S(1)} %get-tuple-element.18) | copy-start | bytes 1572868
  113.0 8.5 %collective-permute-start.13 = (f32[4,128,1]{2,1,0:T(8,128)S(1)}, f32[4,128,1]{2,1,0:T(8,128)S(1)}, u32[]{:S(2)}, u32[]{:S(2)}) collective-permute-start(f32[4,128,1]{2,1,0:T(8,128)S(1)} %get-tuple-element.61), channel_id=1, source_target_pairs={{0,32},{32,64},{64,96},{1,33},{33,65},{65,97},{2,34},{34,66},{66,9... | collective-permute-start | bytes 6152 | tf_op jit(solution)/shard_map/ppermute | solution.py:18
  117.1 8.3 %collective-permute-start.12 = (f32[4,128,1]{2,1,0:T(8,128)S(1)}, f32[4,128,1]{2,1,0:T(8,128)S(1)}, u32[]{:S(2)}, u32[]{:S(2)}) collective-permute-start(f32[4,128,1]{2,1,0:T(8,128)S(1)} %get-tuple-element.62), channel_id=1, source_target_pairs={{32,0},{64,32},{96,64},{33,1},{65,33},{97,65},{34,2},{66,34},{98,6... | collective-permute-start | bytes 6152 | tf_op jit(solution)/shard_map/ppermute | solution.py:19
  125.5 5.6 %collective-permute-start.15 = (f32[4,1,258]{2,1,0:T(1,128)S(1)}, f32[4,1,258]{2,1,0:T(1,128)S(1)}, u32[]{:S(2)}, u32[]{:S(2)}) collective-permute-start(f32[4,1,258]{2,1,0:T(1,128)S(1)} %get-tuple-element.49), channel_id=1, source_target_pairs={{0,2},{2,4},{4,6},{6,8},{8,10},{10,12},{12,14},{14,16},{16,18},{18... | collective-permute-start | bytes 12392 | tf_op jit(solution)/shard_map/ppermute | solution.py:18
  129.5 4.5 collective-permute-start.14
  134.3 7.1 %collective-permute-start.16 = (f32[1,130,258]{2,1,0:T(8,128)S(1)}, f32[1,130,258]{2,1,0:T(8,128)S(1)}, u32[]{:S(2)}, u32[]{:S(2)}) collective-permute-start(f32[1,130,258]{2,1,0:T(8,128)S(1)} %get-tuple-element.39), channel_id=1, source_target_pairs={{1,0},{3,2},{5,4},{7,6},{9,8},{11,10},{13,12},{15,14},{17,16},{19,... | collective-permute-start | bytes 402488 | tf_op jit(solution)/shard_map/ppermute | solution.py:19
  139.8 3.4 collective-permute-start.17
  144.1 9.1 %collective-permute-start.19 = (f32[4,128,1]{2,1,0:T(8,128)S(1)}, f32[4,128,1]{2,1,0:T(8,128)S(1)}, u32[]{:S(2)}, u32[]{:S(2)}) collective-permute-start(f32[4,128,1]{2,1,0:T(8,128)S(1)} %get-tuple-element.59), channel_id=1, source_target_pairs={{0,32},{32,64},{64,96},{1,33},{33,65},{65,97},{2,34},{34,66},{66,9... | collective-permute-start | bytes 6152 | tf_op jit(solution)/shard_map/ppermute | solution.py:18
  147.7 9.3 %collective-permute-start.18 = (f32[4,128,1]{2,1,0:T(8,128)S(1)}, f32[4,128,1]{2,1,0:T(8,128)S(1)}, u32[]{:S(2)}, u32[]{:S(2)}) collective-permute-start(f32[4,128,1]{2,1,0:T(8,128)S(1)} %get-tuple-element.60), channel_id=1, source_target_pairs={{32,0},{64,32},{96,64},{33,1},{65,33},{97,65},{34,2},{66,34},{98,6... | collective-permute-start | bytes 6152 | tf_op jit(solution)/shard_map/ppermute | solution.py:19
  157.1 5.2 collective-permute-start.21
  160.7 6.5 %collective-permute-start.20 = (f32[4,1,258]{2,1,0:T(1,128)S(1)}, f32[4,1,258]{2,1,0:T(1,128)S(1)}, u32[]{:S(2)}, u32[]{:S(2)}) collective-permute-start(f32[4,1,258]{2,1,0:T(1,128)S(1)} %get-tuple-element.48), channel_id=1, source_target_pairs={{2,0},{4,2},{6,4},{8,6},{10,8},{12,10},{14,12},{16,14},{18,16},{20... | collective-permute-start | bytes 12392 | tf_op jit(solution)/shard_map/ppermute | solution.py:19
  167.4 6.1 %collective-permute-start.22 = (f32[1,130,258]{2,1,0:T(8,128)S(1)}, f32[1,130,258]{2,1,0:T(8,128)S(1)}, u32[]{:S(2)}, u32[]{:S(2)}) collective-permute-start(f32[1,130,258]{2,1,0:T(8,128)S(1)} %get-tuple-element.37), channel_id=1, source_target_pairs={{1,0},{3,2},{5,4},{7,6},{9,8},{11,10},{13,12},{15,14},{17,16},{19,... | collective-permute-start | bytes 402488 | tf_op jit(solution)/shard_map/ppermute | solution.py:19
  171.7 3.4 collective-permute-start.23
  230.6 8.6 %collective-permute-start.25 = (f32[4,128,1]{2,1,0:T(8,128)S(1)}, f32[4,128,1]{2,1,0:T(8,128)S(1)}, u32[]{:S(2)}, u32[]{:S(2)}) collective-permute-start(f32[4,128,1]{2,1,0:T(8,128)S(1)} %get-tuple-element.57), channel_id=1, source_target_pairs={{0,32},{32,64},{64,96},{1,33},{33,65},{65,97},{2,34},{34,66},{66,9... | collective-permute-start | bytes 6152 | tf_op jit(solution)/shard_map/ppermute | solution.py:18
  233.8 9.2 %collective-permute-start.24 = (f32[4,128,1]{2,1,0:T(8,128)S(1)}, f32[4,128,1]{2,1,0:T(8,128)S(1)}, u32[]{:S(2)}, u32[]{:S(2)}) collective-permute-start(f32[4,128,1]{2,1,0:T(8,128)S(1)} %get-tuple-element.58), channel_id=1, source_target_pairs={{32,0},{64,32},{96,64},{33,1},{65,33},{97,65},{34,2},{66,34},{98,6... | collective-permute-start | bytes 6152 | tf_op jit(solution)/shard_map/ppermute | solution.py:19
  243.1 7.3 %collective-permute-start.27 = (f32[4,1,258]{2,1,0:T(1,128)S(1)}, f32[4,1,258]{2,1,0:T(1,128)S(1)}, u32[]{:S(2)}, u32[]{:S(2)}) collective-permute-start(f32[4,1,258]{2,1,0:T(1,128)S(1)} %get-tuple-element.45), channel_id=1, source_target_pairs={{0,2},{2,4},{4,6},{6,8},{8,10},{10,12},{12,14},{14,16},{16,18},{18... | collective-permute-start | bytes 12392 | tf_op jit(solution)/shard_map/ppermute | solution.py:18
  248.9 4.7 collective-permute-start.26
  253.8 6.0 %collective-permute-start.28 = (f32[1,130,258]{2,1,0:T(8,128)S(1)}, f32[1,130,258]{2,1,0:T(8,128)S(1)}, u32[]{:S(2)}, u32[]{:S(2)}) collective-permute-start(f32[1,130,258]{2,1,0:T(8,128)S(1)} %get-tuple-element.35), channel_id=1, source_target_pairs={{1,0},{3,2},{5,4},{7,6},{9,8},{11,10},{13,12},{15,14},{17,16},{19,... | collective-permute-start | bytes 402488 | tf_op jit(solution)/shard_map/ppermute | solution.py:19
  258.2 3.4 collective-permute-start.29
  265.3 29.5 %collective-permute-start.31 = (f32[4,128,1]{2,1,0:T(8,128)}, f32[4,128,1]{2,1,0:T(8,128)S(1)}, u32[]{:S(2)}, u32[]{:S(2)}) collective-permute-start(f32[4,128,1]{2,1,0:T(8,128)} %get-tuple-element.55), channel_id=1, source_target_pairs={{0,32},{32,64},{64,96},{1,33},{33,65},{65,97},{2,34},{34,66},{66,9... | collective-permute-start | bytes 6152 | tf_op jit(solution)/shard_map/ppermute | solution.py:18
  267.2 27.6 %collective-permute-start.30 = (f32[4,128,1]{2,1,0:T(8,128)}, f32[4,128,1]{2,1,0:T(8,128)}, u32[]{:S(2)}, u32[]{:S(2)}) collective-permute-start(f32[4,128,1]{2,1,0:T(8,128)} %get-tuple-element.56), channel_id=1, source_target_pairs={{32,0},{64,32},{96,64},{33,1},{65,33},{97,65},{34,2},{66,34},{98,6... | collective-permute-start | bytes 6152 | tf_op jit(solution)/shard_map/ppermute | solution.py:19
  295.7 6.3 %collective-permute-start.33 = (f32[4,1,258]{2,1,0:T(1,128)S(1)}, f32[4,1,258]{2,1,0:T(1,128)S(1)}, u32[]{:S(2)}, u32[]{:S(2)}) collective-permute-start(f32[4,1,258]{2,1,0:T(1,128)S(1)} %get-tuple-element.43), channel_id=1, source_target_pairs={{0,2},{2,4},{4,6},{6,8},{8,10},{10,12},{12,14},{14,16},{16,18},{18... | collective-permute-start | bytes 12392 | tf_op jit(solution)/shard_map/ppermute | solution.py:18
  299.4 4.7 collective-permute-start.32
  305.2 5.1 collective-permute-start.34
  308.7 3.4 collective-permute-start.35
  314.1 25.4 %copy-start.5 = (bf16[3000,4]{1,0:T(8,128)(2,1)S(1)}, bf16[3000,4]{1,0:T(8,128)(2,1)}, u32[]{:S(2)}) copy-start(bf16[3000,4]{1,0:T(8,128)(2,1)} %copy-done.4) | copy-start | bytes 72004
  314.1 25.4 %copy-start.16 = (f32[3000,4]{1,0:T(8,128)S(1)}, f32[3000,4]{1,0:T(8,128)}, u32[]{:S(2)}) copy-start(f32[3000,4]{1,0:T(8,128)} %gather_fusion.1) | copy-start | bytes 144004
  339.5 209.1 %copy-start.23 = (f32[3000]{0:T(1024)S(1)}, f32[3000]{0:T(1024)}, u32[]{:S(2)}) copy-start(f32[3000]{0:T(1024)} %param.26) | copy-start | bytes 36004
  (14 other events, 75.1 us)
